TPU v7x, 32 devices: a whole 2x2x4 slice. The times are simulated.
32 devices in a mesh: slab: 16 (over z, y, x), batch: 2 (over core).
Axes of the slice: x: 2, y: 2, z: 4, core: 2. Of those that a mesh axis runs over, the one named last changes fastest.
Arguments:
- field: bfloat16 [2, 16, 128, 256, 128], P('batch', None, 'slab'), may hold values from -6 to 6
- cotangent: bfloat16 [2, 16, 128, 256, 128], P('batch', None, 'slab'), may hold values from -6 to 6
- spectral_weight: bfloat16 [1024, 2, 16, 512], P('slab'), may hold values from -1 to 1
- point_weight: bfloat16 [16, 16], replicated, may hold values from -1.5 to 1.5
- point_bias: float32 [16], replicated, may hold values from -3 to 3
Outputs:
- input_grad: bfloat16 [2, 16, 128, 256, 128], P('batch', None, 'slab')
- grad_spec: float32 [1024, 2, 16, 512], P('slab')
- grad_point: float32 [16, 16], replicated
- grad_bias: float32 [16], replicated
All inputs are finite; a program needn't handle non-finite values.
Results may differ from a plain program's by a relative error of at most 0.018.
Values may be sent and summed in bfloat16 or wider, within the bound.
A program may use at most 192 MiB of HBM per device.

v0:
```python
import functools
import math

import jax
import jax.numpy as jnp
import ml_dtypes
import numpy as np
from jax import lax
from jax.experimental import pallas as pl
from jax.experimental.pallas import tpu as pltpu
from jax.sharding import PartitionSpec as P

MX = 32
MY = 32
MZ = 32
PB = 16
BF = jnp.bfloat16
F32 = jnp.float32
MESH = pl.DeviceIdType.MESH
VMEM = pl.BlockSpec(memory_space=pltpu.VMEM)


def np_freqs(number, length):
    indices = np.arange(number)
    return np.where(indices < number // 2, indices, indices + (length - number))


def np_phase(positions, frequencies, length):
    product = positions[:, None] * frequencies[None, :] % length
    return product.astype(np.float64) * (2.0 * math.pi / length)


def x_tables(n, planes):
    total = n * planes
    phase = np_phase(np.arange(total), np_freqs(MX, total), total)
    cosine, sine = np.cos(phase), np.sin(phase)
    forward = np.stack(
        [np.stack([cosine, -sine], axis=1), np.stack([sine, cosine], axis=1)], axis=0
    )
    inverse = np.stack(
        [np.stack([cosine, -sine], axis=1), np.stack([sine, cosine], axis=1)], axis=0
    )

    def rows(table, copies):
        table = table.reshape(2, n, planes, 2, MX).transpose(1, 0, 2, 3, 4)
        table = table.reshape(n * 2 * planes, 2, 1, MX)
        table = np.broadcast_to(table, (table.shape[0], 2, copies, MX))
        return table.reshape(table.shape[0], 2 * copies * MX).astype(ml_dtypes.bfloat16)

    return jnp.asarray(rows(forward, 4)), jnp.asarray(rows(inverse, 4))


def enter(n, me, bat):
    barrier = pltpu.get_barrier_semaphore()

    def greet(k, carry):
        pl.semaphore_signal(
            barrier, inc=1, device_id={"slab": lax.rem(me + k, n)}, device_id_type=MESH
        )
        return carry

    lax.fori_loop(1, n, greet, 0)
    pl.semaphore_signal(barrier, inc=1, device_id={"batch": 1 - bat}, device_id_type=MESH)
    pl.semaphore_wait(barrier, n)


def peer_copy(n, me, k, source, target, landed, sems):
    to = lax.rem(me + k, n)
    return pltpu.make_async_remote_copy(
        src_ref=source(to),
        dst_ref=target(landed),
        send_sem=sems.at[0, k],
        recv_sem=sems.at[1, k],
        device_id={"slab": to},
        device_id_type=MESH,
    )


def send_all(n, me, source, target, sems):
    def step(k, carry):
        peer_copy(n, me, k, source, target, me, sems).start()
        return carry

    lax.fori_loop(1, n, step, 0)


def wait_all(n, me, source, target, sems):
    def step(k, carry):
        peer_copy(n, me, k, source, target, lax.rem(me - k + n, n), sems).wait()
        return carry

    lax.fori_loop(1, n, step, 0)


def in_halves(source, target, sems):
    lanes = source.shape[2] // 2
    return [
        (
            lambda to, at=pl.ds(h * lanes, lanes): source.at[to, :, at],
            lambda slot, at=pl.ds(h * lanes, lanes): target.at[slot, :, at],
            sems.at[h],
        )
        for h in range(2)
    ]


def block_pairs(count):
    return min(PB, count // 2)


def block_lanes(block, pairs):
    return pl.ds(pl.multiple_of(block * (pairs * 16), 128), pairs * 16)


def four(values):
    return jnp.concatenate([values] * 4, axis=-1)


def expand(planes_ref, slot, block, pairs, table_ref):
    rows = planes_ref.shape[1] * planes_ref.shape[2]
    part = planes_ref[slot, :, :, block_lanes(block, pairs)].reshape(rows, pairs * 16)
    both = lax.dot_general(
        part, table_ref[...], (((0,), (0,)), ((), ())), preferred_element_type=F32
    )
    half = both.shape[1] // 2
    return (
        both[:, :half].reshape(pairs, 16, half),
        both[:, half:].reshape(pairs, 16, half),
    )


def own_mask(channels):
    shape = (channels, channels * MX)
    row = lax.broadcasted_iota(jnp.int32, shape, 0)
    col = lax.broadcasted_iota(jnp.int32, shape, 1)
    low = row * MX
    return jnp.where((col >= low) & (col < low + MX), 1.0, 0.0).astype(F32)


def lane_fold(values):
    quarter = values.shape[-1] // 4
    return (
        values[..., :quarter]
        + values[..., quarter : 2 * quarter]
        + values[..., 2 * quarter : 3 * quarter]
        + values[..., 3 * quarter :]
    )


def contract(first, second, table_ref, out_ref, block, pairs):
    both = jnp.concatenate([lane_fold(first), lane_fold(second)], axis=-1)
    both = both.reshape(pairs * 16, both.shape[-1]).astype(BF)
    result = lax.dot_general(
        table_ref[...], both, (((1,), (1,)), ((), ())), preferred_element_type=F32
    )
    out_ref[:, :, block_lanes(block, pairs)] = result.astype(BF).reshape(
        out_ref.shape[0], out_ref.shape[1], pairs * 16
    )


def pair_places(count, block, pairs):
    wide = max(count // MZ, 1)
    deep = count // wide
    step = pairs // wide
    return [m * deep + block * step + k for k in range(step) for m in range(wide)]


def weight_pair(w_ref, block, pairs):
    places = pair_places(w_ref.shape[0], block, pairs)
    return tuple(
        jnp.stack([w_ref[at, part].astype(F32) for at in places], axis=0) for part in range(2)
    )


def mix_forward(n, scale, s1, w, t, ti, r1, r2, s2, sems, pair):
    me = lax.axis_index("slab")
    bat = lax.axis_index("batch")
    enter(n, me, bat)
    one = in_halves(s1, r1.at[bat], sems.at[0])
    two = in_halves(s2, r2, sems.at[1])
    pairs = block_pairs(w.shape[0])
    blocks = w.shape[0] // pairs // 2
    for h in range(2):
        send_all(n, me, *one[h])
    r1[bat, me] = s1[me]
    cross = pltpu.make_async_remote_copy(
        src_ref=r1.at[bat],
        dst_ref=r1.at[bat],
        send_sem=pair.at[0],
        recv_sem=pair.at[1],
        device_id={"batch": 1 - bat},
        device_id_type=MESH,
    )
    mask = own_mask(16)[None]

    def step(block, carry):
        u0, u1 = expand(r1, bat, block, pairs, t)
        u0, u1 = four(u0 * scale), four(u1 * scale)
        w0, w1 = weight_pair(w, block, pairs)
        v0 = jnp.sum(u0 * w0 - u1 * w1, axis=1, keepdims=True) * mask
        v1 = jnp.sum(u0 * w1 + u1 * w0, axis=1, keepdims=True) * mask
        contract(v0, v1, ti, s2, block, pairs)
        return carry

    for h in range(2):
        wait_all(n, me, *one[h])
        if h == 1:
            cross.start()
        lax.fori_loop(h * blocks, (h + 1) * blocks, step, 0)
        send_all(n, me, *two[h])
    r2[me] = s2[me]
    cross.wait()
    for h in range(2):
        wait_all(n, me, *two[h])


def mix_backward(
    n, scale_f, scale_i, scale_w, s3, part, w, t, ti, r1, grad, r4, total,
    r3, s4, slots, half, sems, pair,
):
    me = lax.axis_index("slab")
    bat = lax.axis_index("batch")
    enter(n, me, bat)
    one = in_halves(s3, r3.at[bat], sems.at[0])
    two = in_halves(s4, r4, sems.at[1])
    small = (lambda to: part, lambda at: slots.at[at], sems.at[2, 0])
    pairs = block_pairs(w.shape[0])
    blocks = w.shape[0] // pairs // 2
    send_all(n, me, *one[0])
    send_all(n, me, *one[1])
    send_all(n, me, *small)
    r3[bat, me] = s3[me]
    slots[me] = part[...]

    def across(source, target, at):
        return pltpu.make_async_remote_copy(
            src_ref=source,
            dst_ref=target,
            send_sem=pair.at[2 * at],
            recv_sem=pair.at[2 * at + 1],
            device_id={"batch": 1 - bat},
            device_id_type=MESH,
        )

    cross = across(r3.at[bat], r3.at[bat], 0)
    mask = own_mask(16)[None]

    def gradient(slot, block):
        d0, d1 = expand(r3, slot, block, pairs, t)
        d0, d1 = four(d0), four(d1)
        d0 = jnp.sum(d0 * mask, axis=1, keepdims=True) * scale_i
        d1 = jnp.sum(d1 * mask, axis=1, keepdims=True) * scale_i
        return d0, d1

    def step(block, carry):
        d0, d1 = gradient(bat, block)
        w0, w1 = weight_pair(w, block, pairs)
        contract(d0 * w0 + d1 * w1, d1 * w0 - d0 * w1, ti, s4, block, pairs)
        return carry

    for h in range(2):
        wait_all(n, me, *one[h])
        if h == 1:
            cross.start()
        lax.fori_loop(h * blocks, (h + 1) * blocks, step, 0)
        send_all(n, me, *two[h])
    r4[me] = s4[me]
    wait_all(n, me, *small)
    summed = slots[0]
    for at in range(1, n):
        summed = summed + slots[at]
    half[bat] = summed
    other = across(half.at[bat], half.at[bat], 1)
    other.start()
    cross.wait()

    def outer(block, carry):
        places = pair_places(w.shape[0], block, pairs)
        first = None
        for slot in range(2):
            u0, u1 = expand(r1, slot, block, pairs, t)
            u0, u1 = four(u0), four(u1)
            d0, d1 = gradient(slot, block)
            d0, d1 = d0 * (scale_f * scale_w), d1 * (scale_f * scale_w)
            real = u0 * d0 + u1 * d1
            imag = u0 * d1 - u1 * d0
            if first is None:
                first = (real, imag)
            else:
                real, imag = first[0] + real, first[1] + imag
                for row, at in enumerate(places):
                    grad[at, 0] = real[row]
                    grad[at, 1] = imag[row]
        return carry

    lax.fori_loop(0, 2 * blocks, outer, 0)
    other.wait()
    total[...] = half[0] + half[1]
    for h in range(2):
        wait_all(n, me, *two[h])


def run_forward(n, scale, s1, w, t, ti):
    shape = jax.ShapeDtypeStruct
    return pl.pallas_call(
        functools.partial(mix_forward, n, scale),
        out_shape=(shape((2,) + s1.shape, BF), shape(s1.shape, BF)),
        in_specs=[VMEM] * 4,
        out_specs=(VMEM, VMEM),
        scratch_shapes=[
            pltpu.VMEM(s1.shape, BF),
            pltpu.SemaphoreType.DMA((2, 2, 2, n)),
            pltpu.SemaphoreType.DMA((2,)),
        ],
        compiler_params=pltpu.CompilerParams(
            collective_id=0, has_side_effects=True, vmem_limit_bytes=40 << 20
        ),
        name="mix_forward",
    )(s1, w, t, ti)


def run_backward(n, scales, s3, part, w, t, ti, r1):
    shape = jax.ShapeDtypeStruct
    return pl.pallas_call(
        functools.partial(mix_backward, n, *scales),
        out_shape=(shape(w.shape, F32), shape(s3.shape, BF), shape(part.shape, F32)),
        in_specs=[VMEM] * 6,
        out_specs=(VMEM, VMEM, VMEM),
        scratch_shapes=[
            pltpu.VMEM((2,) + s3.shape, BF),
            pltpu.VMEM(s3.shape, BF),
            pltpu.VMEM((n,) + part.shape, F32),
            pltpu.VMEM((2,) + part.shape, F32),
            pltpu.SemaphoreType.DMA((3, 2, 2, n)),
            pltpu.SemaphoreType.DMA((4,)),
        ],
        compiler_params=pltpu.CompilerParams(
            collective_id=1, has_side_effects=True, vmem_limit_bytes=48 << 20
        ),
        name="mix_backward",
    )(s3, part, w, t, ti, r1)


def plane_tables(rows_y, rows_z):
    phase_y = np_phase(np.arange(rows_y), np_freqs(MY, rows_y), rows_y)
    phase_z = np_phase(np.arange(rows_z), np.arange(MZ), rows_z)
    cy, sy, cz, sz = np.cos(phase_y), np.sin(phase_y), np.cos(phase_z), np.sin(phase_z)
    forward_y = np.concatenate([cy, -sy], axis=1).T
    inverse_y = np.concatenate([cy, -sy], axis=1)
    forward_z = np.stack([np.stack([cz, -sz], axis=1), np.stack([sz, cz], axis=1)], axis=0)
    forward_z = forward_z.transpose(3, 2, 0, 1).reshape(2 * MZ, 2 * rows_z)
    cz, sz = cz.T, sz.T
    inverse_z = np.stack([np.stack([cz, sz], axis=1), np.stack([-sz, cz], axis=1)], axis=0)
    inverse_z = inverse_z.transpose(1, 0, 2, 3).reshape(2 * MZ, 2 * rows_z)
    return [
        jnp.asarray(v.astype(ml_dtypes.bfloat16))
        for v in (forward_y, forward_z, inverse_z, inverse_y)
    ]


def piece_layout(n):
    count = MY * MZ // n
    wide = max(count // MZ, 1)
    deep = count // wide
    return wide, deep, wide * 16


def pack_planes(acc, kbuf, out):
    planes, n = acc.shape[0], out.shape[0]
    wide, deep, width = piece_layout(n)
    for x in range(planes):
        for g in range(kbuf.shape[0]):
            kbuf[g, pl.ds(x, 2 * MZ, stride=planes), :] = acc[x, :, g * 128 : (g + 1) * 128]
    group = 128 // width
    for j in range(n):
        m0 = j * wide * deep // MZ
        k0 = j * wide * deep % MZ if wide == 1 else 0
        for first in range(0, deep, group):
            parts = [
                kbuf[
                    m0 * 16 // 128,
                    (k0 + first + q) * 2 * planes : (k0 + first + q + 1) * 2 * planes,
                    m0 * 16 % 128 : m0 * 16 % 128 + width,
                ]
                for q in range(group)
            ]
            out[j, :, first * width : first * width + 128] = jnp.concatenate(
                parts, axis=1
            ).astype(BF)


def unpack_planes(received, kbuf, staged):
    planes, n = staged.shape[0], received.shape[0]
    wide, deep, width = piece_layout(n)
    group = 128 // width
    for k in range(MZ):
        owners = [j for j in range(n) if wide > 1 or j % (MZ // deep) == k // deep]
        lane = (k % deep) * width
        low = lane // 128 * 128
        for first in range(0, len(owners), group):
            parts = [
                received[j, :, low : low + 128].astype(F32)[:, lane - low : lane - low + width]
                for j in owners[first : first + group]
            ]
            kbuf[first // group, k * 2 * planes : (k + 1) * 2 * planes, :] = jnp.concatenate(
                parts, axis=1
            )
    for x in range(planes):
        for g in range(kbuf.shape[0]):
            staged[x, :, g * 128 : (g + 1) * 128] = kbuf[
                g, pl.ds(x, 2 * MZ, stride=planes), :
            ].astype(BF)


def plane_forward(source, fy, fz, lines, acc, x):
    channels = source.shape[0]
    rows = 2 * MY
    for c in range(channels):
        lines[pl.ds(c, rows, stride=channels), :] = jnp.dot(
            fy[...], source[c, 0], preferred_element_type=F32
        )
    half = MY * channels
    both = jnp.concatenate([lines[:half].astype(BF), lines[half:].astype(BF)], axis=1)
    acc[x] = lax.dot_general(fz[...], both, (((1,), (1,)), ((), ())), preferred_element_type=F32)


def spread_map(weight, spread, turned):
    size = spread.shape[0]
    place = lax.broadcasted_iota(jnp.int32, (size, weight.shape[0]), 0) >> 4
    lane = lax.broadcasted_iota(jnp.int32, (size, weight.shape[0]), 1)
    copies = jnp.where(place == lane, 1.0, 0.0).astype(BF)
    contracted = 0 if turned else 1
    rows = lax.dot_general(
        copies, weight[...], (((1,), (contracted,)), ((), ())), preferred_element_type=F32
    ).astype(BF)
    full = lax.dot_general(rows, copies, (((1,), (1,)), ((), ())), preferred_element_type=F32)
    row = lax.broadcasted_iota(jnp.int32, (size, size), 0)
    col = lax.broadcasted_iota(jnp.int32, (size, size), 1)
    spread[...] = jnp.where((row & 15) == (col & 15), full, 0.0).astype(BF)


def plane_inverse(staged, iz, iy, factor, lines, pre, x):
    channels = pre.shape[0]
    half = MY * channels
    rolled = factor * lax.dot_general(
        staged[x], iz[...], (((0,), (0,)), ((), ())), preferred_element_type=F32
    )
    lines[:half] = rolled[:, : rolled.shape[1] // 2]
    lines[half:] = rolled[:, rolled.shape[1] // 2 :]
    for c in range(0, channels, 2):
        pieces = []
        for at in (c, c + 1):
            pieces.append(lines[pl.ds(at, 2 * MY, stride=channels), :].astype(BF))
        result = jnp.dot(
            iy[...], jnp.concatenate(pieces, axis=1), preferred_element_type=F32
        )
        pre[c] = result[:, : result.shape[1] // 2]
        pre[c + 1] = result[:, result.shape[1] // 2 :]


def field_forward(field, fy, fz, out, lines, acc, kbuf):
    x = pl.program_id(0)
    plane_forward(field, fy, fz, lines, acc, x)

    @pl.when(x == pl.num_programs(0) - 1)
    def _():
        pack_planes(acc, kbuf, out)


def tile_rows(ref, step):
    parts = []
    for half in range(2):
        at = slice((2 * step + half) * 16, (2 * step + half + 1) * 16)
        value = ref[:, 0, at, :]
        parts.append(value.reshape(value.shape[0] * 16, value.shape[2]))
    return jnp.concatenate(parts, axis=1)


GELU_K = math.sqrt(2.0 / math.pi)
GELU_C = 0.044715


def gelu_slope(value):
    square = value * value
    bent = jnp.tanh(value * (GELU_K + (GELU_K * GELU_C) * square))
    side = value * (0.5 * GELU_K + (1.5 * GELU_K * GELU_C) * square)
    return (1.0 + bent) * (0.5 + (1.0 - bent) * side)


def middle(
    factor, received, field, cot, weight, bias, fy, fz, iz, iy,
    dpre, out, part, lines, acc, kbuf, staged, pre, spread, outer, sums,
):
    x = pl.program_id(0)
    channels = field.shape[0]

    @pl.when(x == 0)
    def _():
        unpack_planes(received, kbuf, staged)
        spread_map(weight, spread, False)
        outer[...] = jnp.zeros_like(outer)
        sums[...] = jnp.zeros_like(sums)

    plane_inverse(staged, iz, iy, factor, lines, pre, x)

    for at in range(field.shape[2] // 32):
        tile = tile_rows(field, at)
        mixed = jnp.dot(spread[...], tile, preferred_element_type=F32)
        width = mixed.shape[1] // 2
        halves = []
        for half in range(2):
            rows = slice((2 * at + half) * 16, (2 * at + half + 1) * 16)
            value = mixed[:, half * width : (half + 1) * width].reshape(channels, 16, width)
            value = value + pre[:, rows, :] + bias[...][:, None, :]
            slope = gelu_slope(value) * cot[:, 0, rows, :].astype(F32)
            rounded = slope.astype(BF)
            dpre[:, 0, rows, :] = rounded
            wide = rounded.astype(F32)
            sums[...] += wide[:, :8] + wide[:, 8:]
            halves.append(rounded.reshape(channels * 16, width))
        outer[...] += lax.dot_general(
            tile, jnp.concatenate(halves, axis=1), (((1,), (1,)), ((), ())),
            preferred_element_type=F32,
        )
    plane_forward(dpre, fy, fz, lines, acc, x)

    @pl.when(x == pl.num_programs(0) - 1)
    def _():
        pack_planes(acc, kbuf, out)
        size = channels * 16
        row = lax.broadcasted_iota(jnp.int32, (size, size), 0)
        col = lax.broadcasted_iota(jnp.int32, (size, size), 1)
        kept = jnp.where((row & 15) == (col & 15), outer[...], 0.0)
        kept = jnp.sum(kept.reshape(channels, 16, size), axis=1)
        place = lax.broadcasted_iota(jnp.int32, (size, 128), 0) >> 4
        lane = lax.broadcasted_iota(jnp.int32, (size, 128), 1)
        gather = jnp.where(place == lane, 1.0, 0.0).astype(F32)
        part[:channels] = jnp.dot(
            kept, gather, preferred_element_type=F32, precision=lax.Precision.HIGHEST
        )
        part[channels:] = jnp.sum(sums[...], axis=1)


def last(factor, received, dpre, weight, iz, iy, grad, lines, kbuf, staged, pre, spread):
    x = pl.program_id(0)
    channels = dpre.shape[0]

    @pl.when(x == 0)
    def _():
        unpack_planes(received, kbuf, staged)
        spread_map(weight, spread, True)

    plane_inverse(staged, iz, iy, factor, lines, pre, x)

    for at in range(dpre.shape[2] // 32):
        mixed = jnp.dot(spread[...], tile_rows(dpre, at), preferred_element_type=F32)
        width = mixed.shape[1] // 2
        for half in range(2):
            rows = slice((2 * at + half) * 16, (2 * at + half + 1) * 16)
            value = mixed[:, half * width : (half + 1) * width].reshape(channels, 16, width)
            grad[:, 0, rows, :] = (value + pre[:, rows, :]).astype(BF)


def whole(array):
    zeros = (0,) * array.ndim
    return pl.BlockSpec(array.shape, lambda x: zeros)


def plane_block(array):
    c, _, y, z = array.shape
    return pl.BlockSpec((c, 1, y, z), lambda x: (0, x, 0, 0))


def scratch(field, *names):
    c, planes, y, z = field.shape
    every = {
        "lines": pltpu.VMEM((2 * MY * c, z), F32),
        "acc": pltpu.VMEM((planes, 2 * MZ, MY * c), F32),
        "kbuf": pltpu.VMEM((MY * c // 128, 2 * MZ * planes, 128), F32),
        "staged": pltpu.VMEM((planes, 2 * MZ, MY * c), BF),
        "pre": pltpu.VMEM((c, y, z), F32),
        "spread": pltpu.VMEM((16 * c, 16 * c), BF),
        "outer": pltpu.VMEM((16 * c, 16 * c), F32),
        "sums": pltpu.VMEM((c, 8, z), F32),
    }
    return [every[name] for name in names]


def params():
    return pltpu.CompilerParams(vmem_limit_bytes=48 << 20)


def run_first(n, field, fy, fz):
    c, planes, _, _ = field.shape
    out = jax.ShapeDtypeStruct((n, 2 * planes, MY * MZ // n * c), BF)
    return pl.pallas_call(
        field_forward,
        grid=(planes,),
        out_shape=out,
        in_specs=[plane_block(field), whole(fy), whole(fz)],
        out_specs=whole(out),
        scratch_shapes=scratch(field, "lines", "acc", "kbuf"),
        compiler_params=params(),
        name="field_forward",
    )(field, fy, fz)


def run_middle(factor, received, field, cot, weight, bias, fy, fz, iz, iy):
    c, planes, _, _ = field.shape
    out = jax.ShapeDtypeStruct(received.shape, BF)
    part = jax.ShapeDtypeStruct((2 * c, 128), F32)
    flat = [weight, bias, fy, fz, iz, iy]
    return pl.pallas_call(
        functools.partial(middle, factor),
        grid=(planes,),
        out_shape=(jax.ShapeDtypeStruct(field.shape, BF), out, part),
        in_specs=[whole(received), plane_block(field), plane_block(cot)] + [whole(v) for v in flat],
        out_specs=(plane_block(field), whole(out), whole(part)),
        scratch_shapes=scratch(
            field, "lines", "acc", "kbuf", "staged", "pre", "spread", "outer", "sums"
        ),
        compiler_params=params(),
        name="middle",
    )(received, field, cot, *flat)


def run_last(factor, received, dpre, weight, iz, iy):
    c, planes, _, _ = dpre.shape
    flat = [weight, iz, iy]
    return pl.pallas_call(
        functools.partial(last, factor),
        grid=(planes,),
        out_shape=jax.ShapeDtypeStruct(dpre.shape, BF),
        in_specs=[whole(received), plane_block(dpre)] + [whole(v) for v in flat],
        out_specs=plane_block(dpre),
        scratch_shapes=scratch(dpre, "lines", "kbuf", "staged", "pre", "spread"),
        compiler_params=params(),
        name="last",
    )(received, dpre, *flat)


def body(field, cotangent, spectral_weight, point_weight, point_bias):
    samples, channels, planes, rows_y, rows_z = field.shape
    n = lax.axis_size("slab")
    total_samples = samples * lax.axis_size("batch")
    cells = n * planes * rows_y * rows_z
    scale_f = 1.0 / math.sqrt(cells)
    scale_i = 1.0 / math.sqrt(MX * MY * MZ)
    scale_p = 1.0 / math.sqrt(total_samples * cells)
    scale_w = math.sqrt(MX * MY * MZ / (total_samples * cells))
    fy, fz, iz, iy = plane_tables(rows_y, rows_z)
    t, ti = x_tables(n, planes)
    f = field.reshape(field.shape[1:])
    cot = cotangent.reshape(cotangent.shape[1:])
    s1 = run_first(n, f, fy, fz)
    r1, r2 = run_forward(n, scale_f, s1, spectral_weight, t, ti)
    bias = point_bias[:, None]
    dpre, s3, part = run_middle(
        scale_i, r2, f, cot, point_weight, bias, fy, fz, iz, iy
    )
    grad_spec, r4, total = run_backward(
        n, (scale_f, scale_i, scale_w), s3, part, spectral_weight, t, ti, r1
    )
    input_grad = run_last(scale_f, r4, dpre, point_weight, iz, iy)
    return (
        input_grad[None],
        grad_spec,
        scale_p * total[:channels, :channels],
        scale_p * jnp.sum(total[channels:], axis=1),
    )


def solution(mesh):
    placed = (
        P("batch", None, "slab", None, None),
        P("batch", None, "slab", None, None),
        P("slab", None, None, None),
        P(),
        P(),
    )
    return jax.shard_map(
        body,
        mesh=mesh,
        in_specs=placed,
        out_specs=(P("batch", None, "slab", None, None), P("slab", None, None, None), P(), P()),
        check_vma=False,
    )
```

profile of v0, /device:TPU:0, one launch (start us, length us, event | category | flops | bytes accessed | tf_op | source)
XLA Modules:
  0.0 122.3 jit_solution(2297169759189617813)
XLA Ops:
  0.6 0.0 copy-start.1
  0.6 0.0 copy-start
  0.7 0.9 copy.15.bias
  1.5 0.0 copy-start.2
  1.5 0.8 copy-done.2
  2.3 0.0 copy-start.5
  2.3 0.8 copy-done.5
  3.1 0.0 copy-start.4
  3.1 0.0 copy-start.6
  3.1 8.6 %field_forward.1.s1 = bf16[16,16,1024]{2,1,0:T(8,128)(2,1)S(1)} custom-call(bf16[16,8,256,128]{3,2,1,0:T(8,128)(2,1)} %bitcast.4, bf16[64,256]{1,0:T(8,128)(2,1)S(1)} %copy-done.5, bf16[64,256]{1,0:T(8,128)(2,1)S(1)} %copy-done.2), custom_call_target="tpu_custom_call" | custom-call | tf_op jit(solution)/shard_map/field_forward/pallas_call | solution.py:596
  11.7 0.0 copy-done.1
  11.7 0.0 copy-done
  11.7 32.5 %mix_forward.1 = (bf16[2,16,16,1024]{3,2,1,0:T(8,128)(2,1)S(1)}, bf16[16,16,1024]{2,1,0:T(8,128)(2,1)S(1)}) custom-call(bf16[16,16,1024]{2,1,0:T(8,128)(2,1)S(1)} %field_forward.1.s1, bf16[64,2,16,512]{3,2,1,0:T(8,128)(2,1)S(1)} %copy-done, bf16[256,256]{1,0:T(8,128)(2,1)S(1)} %copy-done.1, bf16[256,256]{1,0:T(8,128)(2,1)S(1)} %copy-done.1), custom_call_target="tpu_custom_call" | custom-call | tf_op jit(solution)/shard_map/mix_forward/pallas_call | solution.py:305
  44.2 0.0 copy-done.4
  44.2 0.0 copy-done.6
  44.2 0.0 copy-start.3
  44.2 25.6 %middle.1 = (bf16[16,8,256,128]{3,2,1,0:T(8,128)(2,1)}, bf16[16,16,1024]{2,1,0:T(8,128)(2,1)S(1)}, f32[32,128]{1,0:T(8,128)S(1)}) custom-call(bf16[16,16,1024]{2,1,0:T(8,128)(2,1)S(1)} %get-tuple-element.12.received, bf16[16,8,256,128]{3,2,1,0:T(8,128)(2,1)} %bitcast.5, bf16[16,8,256,128]{3,2,1,0:T(8,128)(2,1)} %bitcast.7, bf16[16,16]{1,0:T(8,128)(2,1)S(1)} %copy-done.6, ...), custom_call_target="tpu_custom_call" | custom-call | tf_op jit(solution)/shard_map/middle/pallas_call | solution.py:613
  69.8 35.8 %mix_backward.1 = (f32[64,2,16,512]{3,2,1,0:T(8,128)}, bf16[16,16,1024]{2,1,0:T(8,128)(2,1)S(1)}, f32[32,128]{1,0:T(8,128)S(1)}) custom-call(bf16[16,16,1024]{2,1,0:T(8,128)(2,1)S(1)} %get-tuple-element.13.s3, f32[32,128]{1,0:T(8,128)S(1)} %get-tuple-element.14.part, bf16[64,2,16,512]{3,2,1,0:T(8,128)(2,1)S(1)} %copy-done, bf16[256,256]{1,0:T(8,128)(2,1)S(1)} %copy-done.1, ...), custom_call_target="tpu_custom_call" | custom-call | tf_op jit(solution)/shard_map/mix_backward/pallas_call | solution.py:324
  105.6 0.0 copy-done.3
  105.6 0.0 copy-start.7
  105.6 13.5 %last.1 = bf16[16,8,256,128]{3,2,1,0:T(8,128)(2,1)} custom-call(bf16[16,16,1024]{2,1,0:T(8,128)(2,1)S(1)} %get-tuple-element.16.received, bf16[16,8,256,128]{3,2,1,0:T(8,128)(2,1)} %get-tuple-element.17.dpre, bf16[16,16]{1,0:T(8,128)(2,1)S(1)} %copy-done.6, bf16[64,256]{1,0:T(8,128)(2,1)S(1)} %copy-done.3, bf16[256,64]{1,0:T(8,128)(2,1)S(1)} %copy-done.4), custom_call_target="tpu_custom_call" | custom-call | tf_op jit(solution)/shard_map/last/pallas_call | solution.py:630
  119.1 0.1 slice_reduce_fusion
  119.2 0.6 slice_multiply_fusion
  119.8 0.5 broadcast_multiply_fusion
  120.3 0.0 copy-done.7
  120.3 2.0 %copy.17 = f32[64,2,16,512]{3,2,1,0:T(8,128)} copy(f32[64,2,16,512]{3,2,1,0:T(8,128)S(1)} %copy-done.7) | data formatting | bytes 8388608
Async XLA Ops:
  0.6 11.1 %copy-start.1 = (bf16[256,256]{1,0:T(8,128)(2,1)S(1)}, bf16[256,256]{1,0:T(8,128)(2,1)}, u32[]{:S(2)}) copy-start(bf16[256,256]{1,0:T(8,128)(2,1)} %constant.16.clone.t.ti) | copy-start | bytes 393220
  0.6 11.1 %copy-start = (bf16[64,2,16,512]{3,2,1,0:T(8,128)(2,1)S(1)}, bf16[64,2,16,512]{3,2,1,0:T(8,128)(2,1)}, u32[]{:S(2)}) copy-start(bf16[64,2,16,512]{3,2,1,0:T(8,128)(2,1)} %w.3) | copy-start | bytes 6291460
  1.5 0.8 copy-start.2
  2.3 0.8 copy-start.5
  3.1 41.2 %copy-start.4 = (bf16[256,64]{1,0:T(8,128)(2,1)S(1)}, bf16[256,64]{1,0:T(8,128)(2,1)}, u32[]{:S(2)}) copy-start(bf16[256,64]{1,0:T(8,128)(2,1)} %constant.15.clone.iy) | copy-start | bytes 98308
  3.1 41.2 %copy-start.6 = (bf16[16,16]{1,0:T(8,128)(2,1)S(1)}, bf16[16,16]{1,0:T(8,128)(2,1)}, u32[]{:S(2)}) copy-start(bf16[16,16]{1,0:T(8,128)(2,1)} %weight.3) | copy-start | bytes 1540
  44.2 61.3 %copy-start.3 = (bf16[64,256]{1,0:T(8,128)(2,1)S(1)}, bf16[64,256]{1,0:T(8,128)(2,1)}, u32[]{:S(2)}) copy-start(bf16[64,256]{1,0:T(8,128)(2,1)} %constant.14.clone.fz.iz) | copy-start | bytes 98308
  105.6 14.7 %copy-start.7 = (f32[64,2,16,512]{3,2,1,0:T(8,128)S(1)}, f32[64,2,16,512]{3,2,1,0:T(8,128)}, u32[]{:S(2)}) copy-start(f32[64,2,16,512]{3,2,1,0:T(8,128)} %get-tuple-element.25) | copy-start | bytes 12582916
where the time goes:
time: 123 us; the launch traced here: 122 us
  Pallas kernels  116 us (94%)
  local copies, waits for them, and re-layouts  4.44 us (4%)
  other arithmetic  1.23 us (1%)
    pallas_call x1, Pallas kernels, run_backward(): pl.pallas_call(functools.partial(mix_backward, n, *scales), out_shape=(sh...  35.8 us
    pallas_call x1, Pallas kernels, run_forward(): pl.pallas_call(functools.partial(mix_forward, n, scale), out_shape=(shape...  32.5 us
    pallas_call x1, Pallas kernels, run_middle(): pl.pallas_call(functools.partial(middle, factor), grid=(planes,), out_sha...  25.6 us
    pallas_call x1, Pallas kernels, run_last(): pl.pallas_call(functools.partial(last, factor), grid=(planes,), out_shape...  13.5 us
    pallas_call x1, Pallas kernels, run_first(): pl.pallas_call(field_forward, grid=(planes,), out_shape=out, in_specs=[pl...  8.63 us
    unnamed x17, local copies, waits for them, and re-layouts  3.56 us

commit v1 on v0

--- a/solution.py
+++ b/solution.py
@@ -77,11 +77,12 @@
 
 
 def send_all(n, me, source, target, sems):
-    def step(k, carry):
+    def step(i, carry):
+        k = n // 2 + (i + 1) // 2 * (2 * (i % 2) - 1)
         peer_copy(n, me, k, source, target, me, sems).start()
         return carry
 
-    lax.fori_loop(1, n, step, 0)
+    lax.fori_loop(0, n - 1, step, 0)
 
 
 def wait_all(n, me, source, target, sems):
@@ -352,10 +353,13 @@
     cz, sz = cz.T, sz.T
     inverse_z = np.stack([np.stack([cz, sz], axis=1), np.stack([-sz, cz], axis=1)], axis=0)
     inverse_z = inverse_z.transpose(1, 0, 2, 3).reshape(2 * MZ, 2 * rows_z)
-    return [
-        jnp.asarray(v.astype(ml_dtypes.bfloat16))
-        for v in (forward_y, forward_z, inverse_z, inverse_y)
-    ]
+    rows = np.concatenate([forward_y, forward_z, inverse_z], axis=0)
+    return [jnp.asarray(v.astype(ml_dtypes.bfloat16)) for v in (rows, inverse_y)]
+
+
+def table_rows(tables):
+    size = tables.shape[0] // 3
+    return [tables[k * size : (k + 1) * size] for k in range(3)]
 
 
 def piece_layout(n):
@@ -415,13 +419,15 @@
 def plane_forward(source, fy, fz, lines, acc, x):
     channels = source.shape[0]
     rows = 2 * MY
-    for c in range(channels):
-        lines[pl.ds(c, rows, stride=channels), :] = jnp.dot(
-            fy[...], source[c, 0], preferred_element_type=F32
-        )
+    for c in range(0, channels, 2):
+        couple = jnp.concatenate([source[c, 0], source[c + 1, 0]], axis=1)
+        result = jnp.dot(fy, couple, preferred_element_type=F32)
+        half = result.shape[1] // 2
+        lines[pl.ds(c, rows, stride=channels), :] = result[:, :half]
+        lines[pl.ds(c + 1, rows, stride=channels), :] = result[:, half:]
     half = MY * channels
     both = jnp.concatenate([lines[:half].astype(BF), lines[half:].astype(BF)], axis=1)
-    acc[x] = lax.dot_general(fz[...], both, (((1,), (1,)), ((), ())), preferred_element_type=F32)
+    acc[x] = lax.dot_general(fz, both, (((1,), (1,)), ((), ())), preferred_element_type=F32)
 
 
 def spread_map(weight, spread, turned):
@@ -443,7 +449,7 @@
     channels = pre.shape[0]
     half = MY * channels
     rolled = factor * lax.dot_general(
-        staged[x], iz[...], (((0,), (0,)), ((), ())), preferred_element_type=F32
+        staged[x], iz, (((0,), (0,)), ((), ())), preferred_element_type=F32
     )
     lines[:half] = rolled[:, : rolled.shape[1] // 2]
     lines[half:] = rolled[:, rolled.shape[1] // 2 :]
@@ -458,8 +464,9 @@
         pre[c + 1] = result[:, result.shape[1] // 2 :]
 
 
-def field_forward(field, fy, fz, out, lines, acc, kbuf):
+def field_forward(field, tables, out, lines, acc, kbuf):
     x = pl.program_id(0)
+    fy, fz, _ = table_rows(tables)
     plane_forward(field, fy, fz, lines, acc, x)
 
     @pl.when(x == pl.num_programs(0) - 1)
@@ -488,16 +495,21 @@
 
 
 def middle(
-    factor, received, field, cot, weight, bias, fy, fz, iz, iy,
-    dpre, out, part, lines, acc, kbuf, staged, pre, spread, outer, sums,
+    factor, received, field, cot, weight, bias, tables, iy,
+    dpre, out, part, lines, acc, kbuf, staged, pre, spread, outer, sums, shift,
 ):
     x = pl.program_id(0)
+    fy, fz, iz = table_rows(tables)
     channels = field.shape[0]
 
     @pl.when(x == 0)
     def _():
         unpack_planes(received, kbuf, staged)
         spread_map(weight, spread, False)
+        row = lax.broadcasted_iota(jnp.int32, (channels, channels), 0)
+        col = lax.broadcasted_iota(jnp.int32, (channels, channels), 1)
+        column = jnp.sum(jnp.where(row == col, bias[...], 0.0), axis=1, keepdims=True)
+        shift[...] = jnp.broadcast_to(column, shift.shape)
         outer[...] = jnp.zeros_like(outer)
         sums[...] = jnp.zeros_like(sums)
 
@@ -511,7 +523,7 @@
         for half in range(2):
             rows = slice((2 * at + half) * 16, (2 * at + half + 1) * 16)
             value = mixed[:, half * width : (half + 1) * width].reshape(channels, 16, width)
-            value = value + pre[:, rows, :] + bias[...][:, None, :]
+            value = value + pre[:, rows, :] + shift[...][:, None, :]
             slope = gelu_slope(value) * cot[:, 0, rows, :].astype(F32)
             rounded = slope.astype(BF)
             dpre[:, 0, rows, :] = rounded
@@ -541,8 +553,9 @@
         part[channels:] = jnp.sum(sums[...], axis=1)
 
 
-def last(factor, received, dpre, weight, iz, iy, grad, lines, kbuf, staged, pre, spread):
+def last(factor, received, dpre, weight, tables, iy, grad, lines, kbuf, staged, pre, spread):
     x = pl.program_id(0)
+    iz = table_rows(tables)[2]
     channels = dpre.shape[0]
 
     @pl.when(x == 0)
@@ -581,6 +594,7 @@
         "pre": pltpu.VMEM((c, y, z), F32),
         "spread": pltpu.VMEM((16 * c, 16 * c), BF),
         "outer": pltpu.VMEM((16 * c, 16 * c), F32),
+        "shift": pltpu.VMEM((c, z), F32),
         "sums": pltpu.VMEM((c, 8, z), F32),
     }
     return [every[name] for name in names]
@@ -590,26 +604,26 @@
     return pltpu.CompilerParams(vmem_limit_bytes=48 << 20)
 
 
-def run_first(n, field, fy, fz):
+def run_first(n, field, tables):
     c, planes, _, _ = field.shape
     out = jax.ShapeDtypeStruct((n, 2 * planes, MY * MZ // n * c), BF)
     return pl.pallas_call(
         field_forward,
         grid=(planes,),
         out_shape=out,
-        in_specs=[plane_block(field), whole(fy), whole(fz)],
+        in_specs=[plane_block(field), whole(tables)],
         out_specs=whole(out),
         scratch_shapes=scratch(field, "lines", "acc", "kbuf"),
         compiler_params=params(),
         name="field_forward",
-    )(field, fy, fz)
-
-
-def run_middle(factor, received, field, cot, weight, bias, fy, fz, iz, iy):
+    )(field, tables)
+
+
+def run_middle(factor, received, field, cot, weight, bias, tables, iy):
     c, planes, _, _ = field.shape
     out = jax.ShapeDtypeStruct(received.shape, BF)
     part = jax.ShapeDtypeStruct((2 * c, 128), F32)
-    flat = [weight, bias, fy, fz, iz, iy]
+    flat = [weight, bias, tables, iy]
     return pl.pallas_call(
         functools.partial(middle, factor),
         grid=(planes,),
@@ -617,16 +631,16 @@
         in_specs=[whole(received), plane_block(field), plane_block(cot)] + [whole(v) for v in flat],
         out_specs=(plane_block(field), whole(out), whole(part)),
         scratch_shapes=scratch(
-            field, "lines", "acc", "kbuf", "staged", "pre", "spread", "outer", "sums"
+            field, "lines", "acc", "kbuf", "staged", "pre", "spread", "outer", "sums", "shift"
         ),
         compiler_params=params(),
         name="middle",
     )(received, field, cot, *flat)
 
 
-def run_last(factor, received, dpre, weight, iz, iy):
+def run_last(factor, received, dpre, weight, tables, iy):
     c, planes, _, _ = dpre.shape
-    flat = [weight, iz, iy]
+    flat = [weight, tables, iy]
     return pl.pallas_call(
         functools.partial(last, factor),
         grid=(planes,),
@@ -648,20 +662,20 @@
     scale_i = 1.0 / math.sqrt(MX * MY * MZ)
     scale_p = 1.0 / math.sqrt(total_samples * cells)
     scale_w = math.sqrt(MX * MY * MZ / (total_samples * cells))
-    fy, fz, iz, iy = plane_tables(rows_y, rows_z)
+    tables, iy = plane_tables(rows_y, rows_z)
     t, ti = x_tables(n, planes)
     f = field.reshape(field.shape[1:])
     cot = cotangent.reshape(cotangent.shape[1:])
-    s1 = run_first(n, f, fy, fz)
+    s1 = run_first(n, f, tables)
     r1, r2 = run_forward(n, scale_f, s1, spectral_weight, t, ti)
-    bias = point_bias[:, None]
+    bias = point_bias[None, :]
     dpre, s3, part = run_middle(
-        scale_i, r2, f, cot, point_weight, bias, fy, fz, iz, iy
+        scale_i, r2, f, cot, point_weight, bias, tables, iy
     )
     grad_spec, r4, total = run_backward(
         n, (scale_f, scale_i, scale_w), s3, part, spectral_weight, t, ti, r1
     )
-    input_grad = run_last(scale_f, r4, dpre, point_weight, iz, iy)
+    input_grad = run_last(scale_f, r4, dpre, point_weight, tables, iy)
     return (
         input_grad[None],
         grad_spec,

time: 123 us -> 120 us (0.976)
  local copies, waits for them, and re-layouts: 4.44 us -> 3.08 us
    unnamed x17 -> x15, local copies, waits for them, and re-layouts: 3.56 us -> 3.08 us
where the time goes in v1:
time: 120 us
  Pallas kernels  115 us (96%)
  local copies, waits for them, and re-layouts  3.08 us (3%)
  other arithmetic  1.23 us (1%)
    pallas_call x1, Pallas kernels, run_backward(): pl.pallas_call(functools.partial(mix_backward, n, *scales), out_shape=(sh...  35.1 us
    pallas_call x1, Pallas kernels, run_forward(): pl.pallas_call(functools.partial(mix_forward, n, scale), out_shape=(shape...  32.2 us
    pallas_call x1, Pallas kernels, run_middle(): pl.pallas_call(functools.partial(middle, factor), grid=(planes,), out_sha...  25.4 us
    pallas_call x1, Pallas kernels, run_last(): pl.pallas_call(functools.partial(last, factor), grid=(planes,), out_shape...  13.5 us
    pallas_call x1, Pallas kernels, run_first(): pl.pallas_call(field_forward, grid=(planes,), out_shape=out, in_specs=[pl...  8.59 us
    unnamed x15, local copies, waits for them, and re-layouts  3.08 us

profile of v1, /device:TPU:0, one launch (start us, length us, event | category | flops | bytes accessed | tf_op | source)
XLA Modules:
  0.0 119.8 jit_solution(3705442415900242672)
XLA Ops:
  0.6 0.0 copy-start.1
  0.6 0.0 copy-start
  0.7 0.0 copy-start.2
  0.7 1.0 copy-done.2
  1.7 0.0 copy-start.3
  1.7 0.0 copy-start.4
  1.7 0.0 copy-start.5
  1.7 8.6 %field_forward.1.s1 = bf16[16,16,1024]{2,1,0:T(8,128)(2,1)S(1)} custom-call(bf16[16,8,256,128]{3,2,1,0:T(8,128)(2,1)} %bitcast.5, bf16[192,256]{1,0:T(8,128)(2,1)S(1)} %copy-done.2), custom_call_target="tpu_custom_call" | custom-call | tf_op jit(solution)/shard_map/field_forward/pallas_call | solution.py:610
  10.3 0.0 copy-done.1
  10.3 0.0 copy-done
  10.3 32.2 %mix_forward.1 = (bf16[2,16,16,1024]{3,2,1,0:T(8,128)(2,1)S(1)}, bf16[16,16,1024]{2,1,0:T(8,128)(2,1)S(1)}) custom-call(bf16[16,16,1024]{2,1,0:T(8,128)(2,1)S(1)} %field_forward.1.s1, bf16[64,2,16,512]{3,2,1,0:T(8,128)(2,1)S(1)} %copy-done, bf16[256,256]{1,0:T(8,128)(2,1)S(1)} %copy-done.1, bf16[256,256]{1,0:T(8,128)(2,1)S(1)} %copy-done.1), custom_call_target="tpu_custom_call" | custom-call | tf_op jit(solution)/shard_map/mix_forward/pallas_call | solution.py:306
  42.5 0.0 copy-done.3
  42.5 0.0 copy-done.4
  42.5 0.0 copy-done.5
  42.5 25.4 %middle.1 = (bf16[16,8,256,128]{3,2,1,0:T(8,128)(2,1)}, bf16[16,16,1024]{2,1,0:T(8,128)(2,1)S(1)}, f32[32,128]{1,0:T(8,128)S(1)}) custom-call(bf16[16,16,1024]{2,1,0:T(8,128)(2,1)S(1)} %get-tuple-element.12.received, bf16[16,8,256,128]{3,2,1,0:T(8,128)(2,1)} %bitcast.6, bf16[16,8,256,128]{3,2,1,0:T(8,128)(2,1)} %bitcast.8, bf16[16,16]{1,0:T(8,128)(2,1)S(1)} %copy-done.4, ...), custom_call_target="tpu_custom_call" | custom-call | tf_op jit(solution)/shard_map/middle/pallas_call | solution.py:627
  67.9 35.1 %mix_backward.1 = (f32[64,2,16,512]{3,2,1,0:T(8,128)}, bf16[16,16,1024]{2,1,0:T(8,128)(2,1)S(1)}, f32[32,128]{1,0:T(8,128)S(1)}) custom-call(bf16[16,16,1024]{2,1,0:T(8,128)(2,1)S(1)} %get-tuple-element.13.s3, f32[32,128]{1,0:T(8,128)S(1)} %get-tuple-element.14.part, bf16[64,2,16,512]{3,2,1,0:T(8,128)(2,1)S(1)} %copy-done, bf16[256,256]{1,0:T(8,128)(2,1)S(1)} %copy-done.1, ...), custom_call_target="tpu_custom_call" | custom-call | tf_op jit(solution)/shard_map/mix_backward/pallas_call | solution.py:325
  103.0 0.0 copy-start.6
  103.0 13.5 %last.1 = bf16[16,8,256,128]{3,2,1,0:T(8,128)(2,1)} custom-call(bf16[16,16,1024]{2,1,0:T(8,128)(2,1)S(1)} %get-tuple-element.16.received, bf16[16,8,256,128]{3,2,1,0:T(8,128)(2,1)} %get-tuple-element.17.dpre, bf16[16,16]{1,0:T(8,128)(2,1)S(1)} %copy-done.4, bf16[192,256]{1,0:T(8,128)(2,1)S(1)} %copy-done.2, bf16[256,64]{1,0:T(8,128)(2,1)S(1)} %copy-done.3), custom_call_target="tpu_custom_call" | custom-call | tf_op jit(solution)/shard_map/last/pallas_call | solution.py:644
  116.5 0.1 slice_reduce_fusion
  116.7 0.6 slice_multiply_fusion
  117.3 0.5 broadcast_multiply_fusion
  117.8 0.0 copy-done.6
  117.8 2.0 %copy.14 = f32[64,2,16,512]{3,2,1,0:T(8,128)} copy(f32[64,2,16,512]{3,2,1,0:T(8,128)S(1)} %copy-done.6) | data formatting | bytes 8388608
Async XLA Ops:
  0.6 9.7 %copy-start.1 = (bf16[256,256]{1,0:T(8,128)(2,1)S(1)}, bf16[256,256]{1,0:T(8,128)(2,1)}, u32[]{:S(2)}) copy-start(bf16[256,256]{1,0:T(8,128)(2,1)} %constant.13.clone.t.ti) | copy-start | bytes 393220
  0.6 9.7 %copy-start = (bf16[64,2,16,512]{3,2,1,0:T(8,128)(2,1)S(1)}, bf16[64,2,16,512]{3,2,1,0:T(8,128)(2,1)}, u32[]{:S(2)}) copy-start(bf16[64,2,16,512]{3,2,1,0:T(8,128)(2,1)} %w.3) | copy-start | bytes 6291460
  0.7 1.0 copy-start.2
  1.7 40.8 %copy-start.3 = (bf16[256,64]{1,0:T(8,128)(2,1)S(1)}, bf16[256,64]{1,0:T(8,128)(2,1)}, u32[]{:S(2)}) copy-start(bf16[256,64]{1,0:T(8,128)(2,1)} %constant.12.clone.iy) | copy-start | bytes 98308
  1.7 40.8 %copy-start.4 = (bf16[16,16]{1,0:T(8,128)(2,1)S(1)}, bf16[16,16]{1,0:T(8,128)(2,1)}, u32[]{:S(2)}) copy-start(bf16[16,16]{1,0:T(8,128)(2,1)} %weight.3) | copy-start | bytes 1540
  1.7 40.8 %copy-start.5 = (f32[16]{0:T(128)S(1)}, f32[16]{0:T(128)}, u32[]{:S(2)}) copy-start(f32[16]{0:T(128)} %param.13) | copy-start | bytes 196
  103.0 14.8 %copy-start.6 = (f32[64,2,16,512]{3,2,1,0:T(8,128)S(1)}, f32[64,2,16,512]{3,2,1,0:T(8,128)}, u32[]{:S(2)}) copy-start(f32[64,2,16,512]{3,2,1,0:T(8,128)} %get-tuple-element.25) | copy-start | bytes 12582916

commit v2 on v1

--- a/solution.py
+++ b/solution.py
@@ -85,28 +85,41 @@
     lax.fori_loop(0, n - 1, step, 0)
 
 
-def wait_all(n, me, source, target, sems):
+def wait_landed(n, me, source, target, sems):
     def step(k, carry):
-        peer_copy(n, me, k, source, target, lax.rem(me - k + n, n), sems).wait()
+        peer_copy(n, me, k, source, target, lax.rem(me - k + n, n), sems).wait_recv()
         return carry
 
     lax.fori_loop(1, n, step, 0)
 
 
-def in_halves(source, target, sems):
-    lanes = source.shape[2] // 2
+def wait_sent(n, me, source, target, sems):
+    def step(k, carry):
+        peer_copy(n, me, k, source, target, me, sems).wait_send()
+        return carry
+
+    lax.fori_loop(1, n, step, 0)
+
+
+def part_count(lanes):
+    return min(4, lanes // 128)
+
+
+def in_parts(source, target, sems):
+    parts = part_count(source.shape[2])
+    lanes = source.shape[2] // parts
     return [
         (
             lambda to, at=pl.ds(h * lanes, lanes): source.at[to, :, at],
             lambda slot, at=pl.ds(h * lanes, lanes): target.at[slot, :, at],
             sems.at[h],
         )
-        for h in range(2)
+        for h in range(parts)
     ]
 
 
 def block_pairs(count):
-    return min(PB, count // 2)
+    return min(PB, count // part_count(count * 16))
 
 
 def block_lanes(block, pairs):
@@ -177,12 +190,12 @@
     me = lax.axis_index("slab")
     bat = lax.axis_index("batch")
     enter(n, me, bat)
-    one = in_halves(s1, r1.at[bat], sems.at[0])
-    two = in_halves(s2, r2, sems.at[1])
+    one = in_parts(s1, r1.at[bat], sems.at[0])
+    two = in_parts(s2, r2, sems.at[1])
     pairs = block_pairs(w.shape[0])
-    blocks = w.shape[0] // pairs // 2
-    for h in range(2):
-        send_all(n, me, *one[h])
+    blocks = w.shape[0] // pairs // len(one)
+    for each in one:
+        send_all(n, me, *each)
     r1[bat, me] = s1[me]
     cross = pltpu.make_async_remote_copy(
         src_ref=r1.at[bat],
@@ -203,16 +216,19 @@
         contract(v0, v1, ti, s2, block, pairs)
         return carry
 
-    for h in range(2):
-        wait_all(n, me, *one[h])
-        if h == 1:
+    for h in range(len(one)):
+        wait_landed(n, me, *one[h])
+        if h == len(one) - 1:
             cross.start()
         lax.fori_loop(h * blocks, (h + 1) * blocks, step, 0)
         send_all(n, me, *two[h])
     r2[me] = s2[me]
     cross.wait()
-    for h in range(2):
-        wait_all(n, me, *two[h])
+    for each in one:
+        wait_sent(n, me, *each)
+    for each in two:
+        wait_landed(n, me, *each)
+        wait_sent(n, me, *each)
 
 
 def mix_backward(
@@ -222,13 +238,13 @@
     me = lax.axis_index("slab")
     bat = lax.axis_index("batch")
     enter(n, me, bat)
-    one = in_halves(s3, r3.at[bat], sems.at[0])
-    two = in_halves(s4, r4, sems.at[1])
+    one = in_parts(s3, r3.at[bat], sems.at[0])
+    two = in_parts(s4, r4, sems.at[1])
     small = (lambda to: part, lambda at: slots.at[at], sems.at[2, 0])
     pairs = block_pairs(w.shape[0])
-    blocks = w.shape[0] // pairs // 2
-    send_all(n, me, *one[0])
-    send_all(n, me, *one[1])
+    blocks = w.shape[0] // pairs // len(one)
+    for each in one:
+        send_all(n, me, *each)
     send_all(n, me, *small)
     r3[bat, me] = s3[me]
     slots[me] = part[...]
@@ -259,14 +275,15 @@
         contract(d0 * w0 + d1 * w1, d1 * w0 - d0 * w1, ti, s4, block, pairs)
         return carry
 
-    for h in range(2):
-        wait_all(n, me, *one[h])
-        if h == 1:
+    for h in range(len(one)):
+        wait_landed(n, me, *one[h])
+        if h == len(one) - 1:
             cross.start()
         lax.fori_loop(h * blocks, (h + 1) * blocks, step, 0)
         send_all(n, me, *two[h])
     r4[me] = s4[me]
-    wait_all(n, me, *small)
+    wait_landed(n, me, *small)
+    wait_sent(n, me, *small)
     summed = slots[0]
     for at in range(1, n):
         summed = summed + slots[at]
@@ -294,11 +311,14 @@
                     grad[at, 1] = imag[row]
         return carry
 
-    lax.fori_loop(0, 2 * blocks, outer, 0)
+    lax.fori_loop(0, len(one) * blocks, outer, 0)
     other.wait()
     total[...] = half[0] + half[1]
-    for h in range(2):
-        wait_all(n, me, *two[h])
+    for each in one:
+        wait_sent(n, me, *each)
+    for each in two:
+        wait_landed(n, me, *each)
+        wait_sent(n, me, *each)
 
 
 def run_forward(n, scale, s1, w, t, ti):
@@ -310,7 +330,7 @@
         out_specs=(VMEM, VMEM),
         scratch_shapes=[
             pltpu.VMEM(s1.shape, BF),
-            pltpu.SemaphoreType.DMA((2, 2, 2, n)),
+            pltpu.SemaphoreType.DMA((2, 4, 2, n)),
             pltpu.SemaphoreType.DMA((2,)),
         ],
         compiler_params=pltpu.CompilerParams(
@@ -332,7 +352,7 @@
             pltpu.VMEM(s3.shape, BF),
             pltpu.VMEM((n,) + part.shape, F32),
             pltpu.VMEM((2,) + part.shape, F32),
-            pltpu.SemaphoreType.DMA((3, 2, 2, n)),
+            pltpu.SemaphoreType.DMA((3, 4, 2, n)),
             pltpu.SemaphoreType.DMA((4,)),
         ],
         compiler_params=pltpu.CompilerParams(

time: 120 us -> 124 us (1.033)
  Pallas kernels: 115 us -> 119 us
    pallas_call x1, Pallas kernels: 35.1 us -> 37.9 us  [run_backward(): pl.pallas_call(functools.partial(mix_backward, n, *scales), out_shape=(sh...]
where the time goes in v2:
time: 124 us
  Pallas kernels  119 us (96%)
  local copies, waits for them, and re-layouts  3.08 us (2%)
    pallas_call x1, Pallas kernels, run_backward(): pl.pallas_call(functools.partial(mix_backward, n, *scales), out_shape=(sh...  37.9 us
    pallas_call x1, Pallas kernels, run_forward(): pl.pallas_call(functools.partial(mix_forward, n, scale), out_shape=(shape...  33.3 us
    pallas_call x1, Pallas kernels, run_middle(): pl.pallas_call(functools.partial(middle, factor), grid=(planes,), out_sha...  25.4 us
    pallas_call x1, Pallas kernels, run_last(): pl.pallas_call(functools.partial(last, factor), grid=(planes,), out_shape...  13.5 us
    pallas_call x1, Pallas kernels, run_first(): pl.pallas_call(field_forward, grid=(planes,), out_shape=out, in_specs=[pl...  8.59 us
    unnamed x15, local copies, waits for them, and re-layouts  3.08 us

profile of v2, /device:TPU:0, one launch (start us, length us, event | category | flops | bytes accessed | tf_op | source)
XLA Modules:
  0.0 123.7 jit_solution(6761660732890946342)
XLA Ops:
  0.6 0.0 copy-start.1
  0.6 0.0 copy-start
  0.7 0.0 copy-start.2
  0.7 1.0 copy-done.2
  1.7 0.0 copy-start.3
  1.7 0.0 copy-start.4
  1.7 0.0 copy-start.5
  1.7 8.6 %field_forward.1.s1 = bf16[16,16,1024]{2,1,0:T(8,128)(2,1)S(1)} custom-call(bf16[16,8,256,128]{3,2,1,0:T(8,128)(2,1)} %bitcast.5, bf16[192,256]{1,0:T(8,128)(2,1)S(1)} %copy-done.2), custom_call_target="tpu_custom_call" | custom-call | tf_op jit(solution)/shard_map/field_forward/pallas_call | solution.py:630
  10.3 0.0 copy-done.1
  10.3 0.0 copy-done
  10.3 33.3 %mix_forward.1 = (bf16[2,16,16,1024]{3,2,1,0:T(8,128)(2,1)S(1)}, bf16[16,16,1024]{2,1,0:T(8,128)(2,1)S(1)}) custom-call(bf16[16,16,1024]{2,1,0:T(8,128)(2,1)S(1)} %field_forward.1.s1, bf16[64,2,16,512]{3,2,1,0:T(8,128)(2,1)S(1)} %copy-done, bf16[256,256]{1,0:T(8,128)(2,1)S(1)} %copy-done.1, bf16[256,256]{1,0:T(8,128)(2,1)S(1)} %copy-done.1), custom_call_target="tpu_custom_call" | custom-call | tf_op jit(solution)/shard_map/mix_forward/pallas_call | solution.py:326
  43.6 0.0 copy-done.3
  43.7 0.0 copy-done.4
  43.7 0.0 copy-done.5
  43.7 25.4 %middle.1 = (bf16[16,8,256,128]{3,2,1,0:T(8,128)(2,1)}, bf16[16,16,1024]{2,1,0:T(8,128)(2,1)S(1)}, f32[32,128]{1,0:T(8,128)S(1)}) custom-call(bf16[16,16,1024]{2,1,0:T(8,128)(2,1)S(1)} %get-tuple-element.12.received, bf16[16,8,256,128]{3,2,1,0:T(8,128)(2,1)} %bitcast.6, bf16[16,8,256,128]{3,2,1,0:T(8,128)(2,1)} %bitcast.8, bf16[16,16]{1,0:T(8,128)(2,1)S(1)} %copy-done.4, ...), custom_call_target="tpu_custom_call" | custom-call | tf_op jit(solution)/shard_map/middle/pallas_call | solution.py:647
  69.1 37.9 %mix_backward.1 = (f32[64,2,16,512]{3,2,1,0:T(8,128)}, bf16[16,16,1024]{2,1,0:T(8,128)(2,1)S(1)}, f32[32,128]{1,0:T(8,128)S(1)}) custom-call(bf16[16,16,1024]{2,1,0:T(8,128)(2,1)S(1)} %get-tuple-element.13.s3, f32[32,128]{1,0:T(8,128)S(1)} %get-tuple-element.14.part, bf16[64,2,16,512]{3,2,1,0:T(8,128)(2,1)S(1)} %copy-done, bf16[256,256]{1,0:T(8,128)(2,1)S(1)} %copy-done.1, ...), custom_call_target="tpu_custom_call" | custom-call | tf_op jit(solution)/shard_map/mix_backward/pallas_call | solution.py:345
  106.9 0.0 copy-start.6
  106.9 13.5 %last.1 = bf16[16,8,256,128]{3,2,1,0:T(8,128)(2,1)} custom-call(bf16[16,16,1024]{2,1,0:T(8,128)(2,1)S(1)} %get-tuple-element.16.received, bf16[16,8,256,128]{3,2,1,0:T(8,128)(2,1)} %get-tuple-element.17.dpre, bf16[16,16]{1,0:T(8,128)(2,1)S(1)} %copy-done.4, bf16[192,256]{1,0:T(8,128)(2,1)S(1)} %copy-done.2, bf16[256,64]{1,0:T(8,128)(2,1)S(1)} %copy-done.3), custom_call_target="tpu_custom_call" | custom-call | tf_op jit(solution)/shard_map/last/pallas_call | solution.py:664
  120.5 0.1 slice_reduce_fusion
  120.6 0.6 slice_multiply_fusion
  121.2 0.5 broadcast_multiply_fusion
  121.7 0.0 copy-done.6
  121.7 2.0 %copy.14 = f32[64,2,16,512]{3,2,1,0:T(8,128)} copy(f32[64,2,16,512]{3,2,1,0:T(8,128)S(1)} %copy-done.6) | data formatting | bytes 8388608
Async XLA Ops:
  0.6 9.7 %copy-start.1 = (bf16[256,256]{1,0:T(8,128)(2,1)S(1)}, bf16[256,256]{1,0:T(8,128)(2,1)}, u32[]{:S(2)}) copy-start(bf16[256,256]{1,0:T(8,128)(2,1)} %constant.13.clone.t.ti) | copy-start | bytes 393220
  0.6 9.7 %copy-start = (bf16[64,2,16,512]{3,2,1,0:T(8,128)(2,1)S(1)}, bf16[64,2,16,512]{3,2,1,0:T(8,128)(2,1)}, u32[]{:S(2)}) copy-start(bf16[64,2,16,512]{3,2,1,0:T(8,128)(2,1)} %w.3) | copy-start | bytes 6291460
  0.7 1.0 copy-start.2
  1.7 41.9 %copy-start.3 = (bf16[256,64]{1,0:T(8,128)(2,1)S(1)}, bf16[256,64]{1,0:T(8,128)(2,1)}, u32[]{:S(2)}) copy-start(bf16[256,64]{1,0:T(8,128)(2,1)} %constant.12.clone.iy) | copy-start | bytes 98308
  1.7 42.0 %copy-start.4 = (bf16[16,16]{1,0:T(8,128)(2,1)S(1)}, bf16[16,16]{1,0:T(8,128)(2,1)}, u32[]{:S(2)}) copy-start(bf16[16,16]{1,0:T(8,128)(2,1)} %weight.3) | copy-start | bytes 1540
  1.7 42.0 %copy-start.5 = (f32[16]{0:T(128)S(1)}, f32[16]{0:T(128)}, u32[]{:S(2)}) copy-start(f32[16]{0:T(128)} %param.13) | copy-start | bytes 196
  106.9 14.8 %copy-start.6 = (f32[64,2,16,512]{3,2,1,0:T(8,128)S(1)}, f32[64,2,16,512]{3,2,1,0:T(8,128)}, u32[]{:S(2)}) copy-start(f32[64,2,16,512]{3,2,1,0:T(8,128)} %get-tuple-element.25) | copy-start | bytes 12582916

commit v3 on v2

--- a/solution.py
+++ b/solution.py
@@ -102,7 +102,7 @@
 
 
 def part_count(lanes):
-    return min(4, lanes // 128)
+    return min(1, lanes // 128)
 
 
 def in_parts(source, target, sems):

time: 124 us -> 128 us (1.032)
  Pallas kernels: 119 us -> 123 us
    pallas_call x1, Pallas kernels: 33.3 us -> 35.5 us  [run_forward(): pl.pallas_call(functools.partial(mix_forward, n, scale), out_shape=(shape...]
    pallas_call x1, Pallas kernels: 37.9 us -> 39.5 us  [run_backward(): pl.pallas_call(functools.partial(mix_backward, n, *scales), out_shape=(sh...]
where the time goes in v3:
time: 128 us
  Pallas kernels  123 us (96%)
  local copies, waits for them, and re-layouts  3.08 us (2%)
    pallas_call x1, Pallas kernels, run_backward(): pl.pallas_call(functools.partial(mix_backward, n, *scales), out_shape=(sh...  39.5 us
    pallas_call x1, Pallas kernels, run_forward(): pl.pallas_call(functools.partial(mix_forward, n, scale), out_shape=(shape...  35.5 us
    pallas_call x1, Pallas kernels, run_middle(): pl.pallas_call(functools.partial(middle, factor), grid=(planes,), out_sha...  25.4 us
    pallas_call x1, Pallas kernels, run_last(): pl.pallas_call(functools.partial(last, factor), grid=(planes,), out_shape...  13.5 us
    pallas_call x1, Pallas kernels, run_first(): pl.pallas_call(field_forward, grid=(planes,), out_shape=out, in_specs=[pl...  8.59 us
    unnamed x15, local copies, waits for them, and re-layouts  3.08 us

profile of v3, /device:TPU:0, one launch (start us, length us, event | category | flops | bytes accessed | tf_op | source)
XLA Modules:
  0.0 127.6 jit_solution(9708191012558474905)
XLA Ops:
  0.6 0.0 copy-start.1
  0.6 0.0 copy-start
  0.7 0.0 copy-start.2
  0.7 1.0 copy-done.2
  1.7 0.0 copy-start.3
  1.7 0.0 copy-start.4
  1.7 0.0 copy-start.5
  1.7 8.6 %field_forward.1.s1 = bf16[16,16,1024]{2,1,0:T(8,128)(2,1)S(1)} custom-call(bf16[16,8,256,128]{3,2,1,0:T(8,128)(2,1)} %bitcast.5, bf16[192,256]{1,0:T(8,128)(2,1)S(1)} %copy-done.2), custom_call_target="tpu_custom_call" | custom-call | tf_op jit(solution)/shard_map/field_forward/pallas_call | solution.py:630
  10.3 0.0 copy-done.1
  10.3 0.0 copy-done
  10.3 35.5 %mix_forward.1 = (bf16[2,16,16,1024]{3,2,1,0:T(8,128)(2,1)S(1)}, bf16[16,16,1024]{2,1,0:T(8,128)(2,1)S(1)}) custom-call(bf16[16,16,1024]{2,1,0:T(8,128)(2,1)S(1)} %field_forward.1.s1, bf16[64,2,16,512]{3,2,1,0:T(8,128)(2,1)S(1)} %copy-done, bf16[256,256]{1,0:T(8,128)(2,1)S(1)} %copy-done.1, bf16[256,256]{1,0:T(8,128)(2,1)S(1)} %copy-done.1), custom_call_target="tpu_custom_call" | custom-call | tf_op jit(solution)/shard_map/mix_forward/pallas_call | solution.py:326
  45.9 0.0 copy-done.3
  45.9 0.0 copy-done.4
  45.9 0.0 copy-done.5
  45.9 25.4 %middle.1 = (bf16[16,8,256,128]{3,2,1,0:T(8,128)(2,1)}, bf16[16,16,1024]{2,1,0:T(8,128)(2,1)S(1)}, f32[32,128]{1,0:T(8,128)S(1)}) custom-call(bf16[16,16,1024]{2,1,0:T(8,128)(2,1)S(1)} %get-tuple-element.12.received, bf16[16,8,256,128]{3,2,1,0:T(8,128)(2,1)} %bitcast.6, bf16[16,8,256,128]{3,2,1,0:T(8,128)(2,1)} %bitcast.8, bf16[16,16]{1,0:T(8,128)(2,1)S(1)} %copy-done.4, ...), custom_call_target="tpu_custom_call" | custom-call | tf_op jit(solution)/shard_map/middle/pallas_call | solution.py:647
  71.3 39.5 %mix_backward.1 = (f32[64,2,16,512]{3,2,1,0:T(8,128)}, bf16[16,16,1024]{2,1,0:T(8,128)(2,1)S(1)}, f32[32,128]{1,0:T(8,128)S(1)}) custom-call(bf16[16,16,1024]{2,1,0:T(8,128)(2,1)S(1)} %get-tuple-element.13.s3, f32[32,128]{1,0:T(8,128)S(1)} %get-tuple-element.14.part, bf16[64,2,16,512]{3,2,1,0:T(8,128)(2,1)S(1)} %copy-done, bf16[256,256]{1,0:T(8,128)(2,1)S(1)} %copy-done.1, ...), custom_call_target="tpu_custom_call" | custom-call | tf_op jit(solution)/shard_map/mix_backward/pallas_call | solution.py:345
  110.8 0.0 copy-start.6
  110.8 13.5 %last.1 = bf16[16,8,256,128]{3,2,1,0:T(8,128)(2,1)} custom-call(bf16[16,16,1024]{2,1,0:T(8,128)(2,1)S(1)} %get-tuple-element.16.received, bf16[16,8,256,128]{3,2,1,0:T(8,128)(2,1)} %get-tuple-element.17.dpre, bf16[16,16]{1,0:T(8,128)(2,1)S(1)} %copy-done.4, bf16[192,256]{1,0:T(8,128)(2,1)S(1)} %copy-done.2, bf16[256,64]{1,0:T(8,128)(2,1)S(1)} %copy-done.3), custom_call_target="tpu_custom_call" | custom-call | tf_op jit(solution)/shard_map/last/pallas_call | solution.py:664
  124.3 0.1 slice_reduce_fusion
  124.5 0.6 slice_multiply_fusion
  125.1 0.5 broadcast_multiply_fusion
  125.6 0.0 copy-done.6
  125.6 2.0 %copy.14 = f32[64,2,16,512]{3,2,1,0:T(8,128)} copy(f32[64,2,16,512]{3,2,1,0:T(8,128)S(1)} %copy-done.6) | data formatting | bytes 8388608
Async XLA Ops:
  0.6 9.7 %copy-start.1 = (bf16[256,256]{1,0:T(8,128)(2,1)S(1)}, bf16[256,256]{1,0:T(8,128)(2,1)}, u32[]{:S(2)}) copy-start(bf16[256,256]{1,0:T(8,128)(2,1)} %constant.13.clone.t.ti) | copy-start | bytes 393220
  0.6 9.7 %copy-start = (bf16[64,2,16,512]{3,2,1,0:T(8,128)(2,1)S(1)}, bf16[64,2,16,512]{3,2,1,0:T(8,128)(2,1)}, u32[]{:S(2)}) copy-start(bf16[64,2,16,512]{3,2,1,0:T(8,128)(2,1)} %w.3) | copy-start | bytes 6291460
  0.7 1.0 copy-start.2
  1.7 44.2 %copy-start.3 = (bf16[256,64]{1,0:T(8,128)(2,1)S(1)}, bf16[256,64]{1,0:T(8,128)(2,1)}, u32[]{:S(2)}) copy-start(bf16[256,64]{1,0:T(8,128)(2,1)} %constant.12.clone.iy) | copy-start | bytes 98308
  1.7 44.2 %copy-start.4 = (bf16[16,16]{1,0:T(8,128)(2,1)S(1)}, bf16[16,16]{1,0:T(8,128)(2,1)}, u32[]{:S(2)}) copy-start(bf16[16,16]{1,0:T(8,128)(2,1)} %weight.3) | copy-start | bytes 1540
  1.7 44.2 %copy-start.5 = (f32[16]{0:T(128)S(1)}, f32[16]{0:T(128)}, u32[]{:S(2)}) copy-start(f32[16]{0:T(128)} %param.13) | copy-start | bytes 196
  110.8 14.8 %copy-start.6 = (f32[64,2,16,512]{3,2,1,0:T(8,128)S(1)}, f32[64,2,16,512]{3,2,1,0:T(8,128)}, u32[]{:S(2)}) copy-start(f32[64,2,16,512]{3,2,1,0:T(8,128)} %get-tuple-element.25) | copy-start | bytes 12582916
